TPU v7x, 32 devices: a whole 2x2x4 slice. The times are simulated.
32 devices in a mesh: dp: 8 (over z, y), fsdp: 4 (over x, core).
Axes of the slice: x: 2, y: 2, z: 4, core: 2. Of those that a mesh axis runs over, the one named last changes fastest.
Arguments:
- inputs: bfloat16 [64, 512, 768], P(('dp', 'fsdp')), may hold values from -6 to 6
- segment_ids: int32 [64, 512], P(('dp', 'fsdp')), may hold values from 0 to 5, as said below
- compressed_segment: int32 [64, 256], P(('dp', 'fsdp')), may hold values from 0 to 5, as said below
- out_grad: bfloat16 [64, 512, 768], P(('dp', 'fsdp')), may hold values from -6 to 6
- attn_weight: float32 [4, 768, 768], P(None, ('dp', 'fsdp')), may hold values from -1.1549411 to 1.1549411
- attn_first: float32 [4, 768, 768], P(None, ('dp', 'fsdp')), may hold values from -68.787348 to 68.787348
- attn_second: float32 [4, 768, 768], P(None, ('dp', 'fsdp')), may hold values from 0.32768 to 64.22528
- up_weight: float32 [768, 3072], P(('dp', 'fsdp')), may hold values from -0.17681352 to 0.17681352
- up_first: float32 [768, 3072], P(('dp', 'fsdp')), may hold values from -30.773287 to 30.773287
- up_second: float32 [768, 3072], P(('dp', 'fsdp')), may hold values from 2.94912 to 11.79648
- down_weight: float32 [3072, 768], P(('dp', 'fsdp')), may hold values from -0.125026039 to 0.125026039
- down_first: float32 [3072, 768], P(('dp', 'fsdp')), may hold values from -45.254834 to 45.254834
- down_second: float32 [3072, 768], P(('dp', 'fsdp')), may hold values from 6.5536 to 26.2144
- compress_weight: float32 [256, 512], P(('dp', 'fsdp')), may hold values from -0.4331029 to 0.4331029
- compress_first: float32 [256, 512], P(('dp', 'fsdp')), may hold values from -86.4 to 86.4
- compress_second: float32 [256, 512], P(('dp', 'fsdp')), may hold values from 25.6 to 102.4
- norm_params: float32 [4, 768], P(None, ('dp', 'fsdp')), may hold values from -1.2 to 1.5
- norm_first: float32 [4, 768], P(None, ('dp', 'fsdp')), may hold values from -128 to 128
- norm_second: float32 [4, 768], P(None, ('dp', 'fsdp')), may hold values from 32.768 to 131.072
Outputs:
- block_output: bfloat16 [64, 512, 768], P(('dp', 'fsdp'))
- input_grad: float32 [64, 512, 768], P(('dp', 'fsdp'))
- attn_first_new: float32 [4, 768, 768], P(None, ('dp', 'fsdp'))
- attn_second_new: float32 [3, 768, 768], P(None, ('dp', 'fsdp'))
- out_second_new: float32 [768, 768], P(('dp', 'fsdp'))
- attn_new: float32 [4, 768, 768], P(None, ('dp', 'fsdp'))
- attn_copy: bfloat16 [4, 768, 768], P(None, ('dp', 'fsdp'))
- up_first_new: float32 [768, 3072], P(('dp', 'fsdp'))
- up_second_new: float32 [768, 3072], P(('dp', 'fsdp'))
- up_new: float32 [768, 3072], P(('dp', 'fsdp'))
- up_copy: bfloat16 [768, 3072], P(('dp', 'fsdp'))
- down_first_new: float32 [3072, 768], P(('dp', 'fsdp'))
- down_second_new: float32 [3072, 768], P(('dp', 'fsdp'))
- down_new: float32 [3072, 768], P(('dp', 'fsdp'))
- down_copy: bfloat16 [3072, 768], P(('dp', 'fsdp'))
- compress_first_new: float32 [256, 512], P(('dp', 'fsdp'))
- compress_second_new: float32 [256, 512], P(('dp', 'fsdp'))
- compress_new: float32 [256, 512], P(('dp', 'fsdp'))
- compress_copy: bfloat16 [256, 512], P(('dp', 'fsdp'))
- norm_first_new: float32 [4, 768], P(None, ('dp', 'fsdp'))
- norm_second_new: float32 [4, 768], P(None, ('dp', 'fsdp'))
- norm_new: float32 [4, 768], P(None, ('dp', 'fsdp'))
- norms: float32 [2, 7], replicated
Inputs may be any that keep to these rules, and one draw needn't show every extreme that they name: `segment_ids`: along each row the ids start at 0 and never fall; each segment is one run of tokens whose start and length are multiples of 8. `compressed_segment`: along each row the values start at 0, never fall and end at the largest segment id of the same row; every segment of a row owns one or more compressed rows.
All inputs are finite; a program needn't handle non-finite values.
Results may differ from a plain program's by a relative error of at most 0.015.
The roundings to bfloat16 on the way count: a program that leaves them out, or rounds other values in their place, can miss the bound.
Values may be sent and summed in bfloat16 or wider, within the bound.
No kernel may reach another device: no remote copies, remote signals or barrier semaphores. Data moves between devices by JAX's collectives and lax.ppermute only.
A program may use at most 192 MiB of HBM per device.

v0:
```python
import jax
import jax.numpy as jnp
from jax import lax
from jax.sharding import PartitionSpec as P

HEAD_DIM = 64
STEP = 10


BETA_ONE = 0.9
BETA_TWO = 0.999
EPSILON = 1e-06
DECAY = 0.01
RATE = 0.5
NORM_EPS = 1e-05
MASKED = -1e30


def gelu_exact(argument):
    return jax.nn.gelu(argument, approximate=False)


def norm_forward(mixed, gain_row, bias_row):
    average = jnp.mean(mixed, axis=-1, keepdims=True)
    centered = mixed - average
    inv_std = lax.rsqrt(jnp.mean(centered * centered, axis=-1, keepdims=True) + NORM_EPS)
    normalized = centered * inv_std
    return (normalized * gain_row + bias_row, normalized, inv_std)


def norm_backward(grad_out, normalized, inv_std, gain_row):
    scaled = grad_out * gain_row
    grad_in = inv_std * (
        scaled
        - jnp.mean(scaled, axis=-1, keepdims=True)
        - normalized * jnp.mean(scaled * normalized, axis=-1, keepdims=True)
    )
    return (grad_in, jnp.sum(grad_out * normalized, axis=0), jnp.sum(grad_out, axis=0))


def adaptive(first, second, grad):
    first_new = BETA_ONE * first + (1.0 - BETA_ONE) * grad
    second_new = BETA_TWO * second + (1.0 - BETA_TWO) * grad * grad
    direction = (
        first_new
        / (1.0 - BETA_ONE**STEP)
        / (jnp.sqrt(second_new / (1.0 - BETA_TWO**STEP)) + EPSILON)
    )
    return (first_new, second_new, direction)


def matrix_squares(attn_part, up_part, down_part, compress_part):
    return jnp.concatenate(
        [
            jnp.sum(attn_part * attn_part, axis=(1, 2)),
            jnp.stack(
                [
                    jnp.sum(up_part * up_part),
                    jnp.sum(down_part * down_part),
                    jnp.sum(compress_part * compress_part),
                ]
            ),
        ]
    )


def local(
    inputs,
    segment_ids,
    compressed_segment,
    out_grad,
    attn_weight,
    attn_first,
    attn_second,
    up_weight,
    up_first,
    up_second,
    down_weight,
    down_first,
    down_second,
    compress_weight,
    compress_first,
    compress_second,
    norm_params,
    norm_first,
    norm_second,
):
    low_type = jnp.bfloat16
    full_type = jnp.float32
    attn_full, compress_full, norm_full = (
        lax.all_gather(attn_weight.astype(low_type), ("dp", "fsdp"), axis=1, tiled=True),
        lax.all_gather(compress_weight.astype(low_type), ("dp", "fsdp"), axis=0, tiled=True),
        lax.all_gather(norm_params.astype(low_type), ("dp", "fsdp"), axis=1, tiled=True),
    )
    up_full, down_full = (
        lax.all_gather(up_weight.astype(low_type), ("dp", "fsdp"), axis=0, tiled=True),
        lax.all_gather(down_weight.astype(low_type), ("dp", "fsdp"), axis=0, tiled=True),
    )
    gains = norm_full.astype(full_type)
    row_count, length, model_width = inputs.shape
    head_count = model_width // HEAD_DIM
    token_count = row_count * length
    score_scale = HEAD_DIM ** (-0.5)
    flat_in = inputs.reshape(token_count, model_width)
    projected = jnp.einsum(
        "td,jde->jte", flat_in, attn_full[:3], preferred_element_type=full_type
    ).astype(low_type)
    queries = projected[0].reshape(row_count, length, head_count, HEAD_DIM)
    kv_low = projected[1:3].reshape(2, row_count, length, model_width)
    member = compressed_segment[:, :, None] == segment_ids[:, None, :]
    masked_proj = jnp.where(member, compress_full[None], jnp.zeros((), low_type))
    compressed = jnp.einsum(
        "rks,jrsd->jrkd", masked_proj, kv_low, preferred_element_type=full_type
    ).astype(low_type)
    comp_keys = compressed[0].reshape(row_count, -1, head_count, HEAD_DIM)
    comp_values = compressed[1].reshape(row_count, -1, head_count, HEAD_DIM)
    allowed = segment_ids[:, None, :, None] == compressed_segment[:, None, None, :]
    scores = (
        jnp.einsum("rshe,rkhe->rhsk", queries, comp_keys, preferred_element_type=full_type)
        * score_scale
    )
    scores = jnp.where(allowed, scores, MASKED)
    highest = jnp.max(scores, axis=-1, keepdims=True)
    weights = jnp.exp(scores - highest)
    totals = jnp.sum(weights, axis=-1, keepdims=True)
    log_total = highest + jnp.log(totals)
    probs_low = (weights / totals).astype(low_type)
    context = (
        jnp.einsum("rhsk,rkhe->rshe", probs_low, comp_values, preferred_element_type=full_type)
        .astype(low_type)
        .reshape(token_count, model_width)
    )
    attended = jnp.dot(context, attn_full[3], preferred_element_type=full_type)
    first_out, first_normed, first_inv = norm_forward(
        flat_in.astype(full_type) + attended, gains[0], gains[1]
    )
    first_low = first_out.astype(low_type)
    hidden = jnp.dot(first_low, up_full, preferred_element_type=full_type)
    gelu_value, gelu_pull = jax.vjp(gelu_exact, hidden)
    active = gelu_value.astype(low_type)
    branch = jnp.dot(active, down_full, preferred_element_type=full_type)
    second_out, second_normed, second_inv = norm_forward(first_out + branch, gains[2], gains[3])
    result = second_out.astype(low_type).reshape(row_count, length, model_width)
    up_back, down_back = (
        lax.all_gather(up_weight.astype(low_type), ("dp", "fsdp"), axis=0, tiled=True),
        lax.all_gather(down_weight.astype(low_type), ("dp", "fsdp"), axis=0, tiled=True),
    )
    grad_top = out_grad.reshape(token_count, model_width).astype(full_type)
    grad_second, gain_two, bias_two = norm_backward(grad_top, second_normed, second_inv, gains[2])
    grad_second_low = grad_second.astype(low_type)
    down_grad = jnp.einsum("tf,td->fd", active, grad_second_low, preferred_element_type=full_type)
    grad_active = jnp.einsum(
        "td,fd->tf", grad_second_low, down_back, preferred_element_type=full_type
    )
    grad_hidden_low = gelu_pull(grad_active)[0].astype(low_type)
    up_grad = jnp.einsum("td,tf->df", first_low, grad_hidden_low, preferred_element_type=full_type)
    grad_first_out = grad_second + jnp.einsum(
        "tf,df->td", grad_hidden_low, up_back, preferred_element_type=full_type
    )
    attn_back, compress_back = (
        lax.all_gather(attn_weight.astype(low_type), ("dp", "fsdp"), axis=1, tiled=True),
        lax.all_gather(compress_weight.astype(low_type), ("dp", "fsdp"), axis=0, tiled=True),
    )
    masked_back = jnp.where(member, compress_back[None], jnp.zeros((), low_type))
    grad_first, gain_one, bias_one = norm_backward(
        grad_first_out, first_normed, first_inv, gains[0]
    )
    grad_first_low = grad_first.astype(low_type)
    out_proj_grad = jnp.einsum(
        "td,te->de", context, grad_first_low, preferred_element_type=full_type
    )
    grad_context = (
        jnp.einsum("te,de->td", grad_first_low, attn_back[3], preferred_element_type=full_type)
        .astype(low_type)
        .reshape(row_count, length, head_count, HEAD_DIM)
    )
    scores_again = (
        jnp.einsum("rshe,rkhe->rhsk", queries, comp_keys, preferred_element_type=full_type)
        * score_scale
    )
    probability = jnp.exp(jnp.where(allowed, scores_again - log_total, MASKED))
    probs_again = probability.astype(low_type)
    grad_probs = jnp.einsum(
        "rshe,rkhe->rhsk", grad_context, comp_values, preferred_element_type=full_type
    )
    row_delta = jnp.sum(probability * grad_probs, axis=-1, keepdims=True)
    grad_scores = (probability * (grad_probs - row_delta)).astype(low_type)
    grad_queries = (
        jnp.einsum("rhsk,rkhe->rshe", grad_scores, comp_keys, preferred_element_type=full_type)
        * score_scale
    ).astype(low_type)
    grad_comp_keys = (
        jnp.einsum("rhsk,rshe->rkhe", grad_scores, queries, preferred_element_type=full_type)
        * score_scale
    ).astype(low_type)
    grad_comp_values = jnp.einsum(
        "rhsk,rshe->rkhe", probs_again, grad_context, preferred_element_type=full_type
    ).astype(low_type)
    grad_comp = jnp.stack(
        [
            grad_comp_keys.reshape(row_count, -1, model_width),
            grad_comp_values.reshape(row_count, -1, model_width),
        ]
    )
    grad_kv = jnp.einsum(
        "rks,jrkd->jrsd", masked_back, grad_comp, preferred_element_type=full_type
    ).astype(low_type)
    comp_grad = jnp.sum(
        jnp.where(
            member,
            jnp.einsum("jrkd,jrsd->rks", grad_comp, kv_low, preferred_element_type=full_type),
            0.0,
        ),
        axis=0,
    )
    grad_qkv = jnp.concatenate(
        [
            grad_queries.reshape(1, token_count, model_width),
            grad_kv.reshape(2, token_count, model_width),
        ]
    )
    qkv_grad = jnp.einsum("td,jte->jde", flat_in, grad_qkv, preferred_element_type=full_type)
    input_grad = grad_first + jnp.einsum(
        "jte,jde->td", grad_qkv, attn_back[:3], preferred_element_type=full_type
    )
    attn_grad = jnp.concatenate([qkv_grad, out_proj_grad[None]])
    norm_grad = jnp.stack([gain_one, bias_one, gain_two, bias_two])
    up_owned, down_owned, attn_owned, compress_owned, norm_owned = (
        lax.psum_scatter(up_grad, ("dp", "fsdp"), scatter_dimension=0, tiled=True),
        lax.psum_scatter(down_grad, ("dp", "fsdp"), scatter_dimension=0, tiled=True),
        lax.psum_scatter(attn_grad, ("dp", "fsdp"), scatter_dimension=1, tiled=True),
        lax.psum_scatter(comp_grad, ("dp", "fsdp"), scatter_dimension=0, tiled=True),
        lax.psum_scatter(norm_grad, ("dp", "fsdp"), scatter_dimension=1, tiled=True),
    )
    attn_first_new, attn_second_new, attn_direction = adaptive(attn_first, attn_second, attn_owned)
    up_first_new, up_second_new, up_direction = adaptive(up_first, up_second, up_owned)
    down_first_new, down_second_new, down_direction = adaptive(down_first, down_second, down_owned)
    compress_first_new, compress_second_new, compress_direction = adaptive(
        compress_first, compress_second, compress_owned
    )
    norm_first_new, norm_second_new, norm_direction = adaptive(norm_first, norm_second, norm_owned)
    attn_direction = attn_direction + DECAY * attn_weight
    up_direction = up_direction + DECAY * up_weight
    down_direction = down_direction + DECAY * down_weight
    compress_direction = compress_direction + DECAY * compress_weight
    update_sq = matrix_squares(attn_direction, up_direction, down_direction, compress_direction)
    weight_sq, update_total = lax.psum(
        (matrix_squares(attn_weight, up_weight, down_weight, compress_weight), update_sq),
        ("dp", "fsdp"),
    )
    weight_norm = jnp.sqrt(weight_sq)
    update_norm = jnp.sqrt(update_total)
    trust_ratio = weight_norm / (update_norm + EPSILON)
    attn_new = attn_weight - RATE * trust_ratio[:4].reshape(4, 1, 1) * attn_direction
    up_new = up_weight - RATE * trust_ratio[4] * up_direction
    down_new = down_weight - RATE * trust_ratio[5] * down_direction
    compress_new = compress_weight - RATE * trust_ratio[6] * compress_direction
    norm_new = norm_params - RATE * norm_direction
    norms = jnp.stack([weight_norm, update_norm])
    return (
        result,
        input_grad.reshape(row_count, length, model_width),
        attn_first_new,
        attn_second_new[:3],
        attn_second_new[3],
        attn_new,
        attn_new.astype(low_type),
        up_first_new,
        up_second_new,
        up_new,
        up_new.astype(low_type),
        down_first_new,
        down_second_new,
        down_new,
        down_new.astype(low_type),
        compress_first_new,
        compress_second_new,
        compress_new,
        compress_new.astype(low_type),
        norm_first_new,
        norm_second_new,
        norm_new,
        norms,
    )


def solution(mesh):
    return jax.shard_map(
        local,
        mesh=mesh,
        in_specs=(
            P(("dp", "fsdp"), None, None),
            P(("dp", "fsdp"), None),
            P(("dp", "fsdp"), None),
            P(("dp", "fsdp"), None, None),
            P(None, ("dp", "fsdp"), None),
            P(None, ("dp", "fsdp"), None),
            P(None, ("dp", "fsdp"), None),
            P(("dp", "fsdp"), None),
            P(("dp", "fsdp"), None),
            P(("dp", "fsdp"), None),
            P(("dp", "fsdp"), None),
            P(("dp", "fsdp"), None),
            P(("dp", "fsdp"), None),
            P(("dp", "fsdp"), None),
            P(("dp", "fsdp"), None),
            P(("dp", "fsdp"), None),
            P(None, ("dp", "fsdp")),
            P(None, ("dp", "fsdp")),
            P(None, ("dp", "fsdp")),
        ),
        out_specs=(
            P(("dp", "fsdp"), None, None),
            P(("dp", "fsdp"), None, None),
            P(None, ("dp", "fsdp"), None),
            P(None, ("dp", "fsdp"), None),
            P(("dp", "fsdp"), None),
            P(None, ("dp", "fsdp"), None),
            P(None, ("dp", "fsdp"), None),
            P(("dp", "fsdp"), None),
            P(("dp", "fsdp"), None),
            P(("dp", "fsdp"), None),
            P(("dp", "fsdp"), None),
            P(("dp", "fsdp"), None),
            P(("dp", "fsdp"), None),
            P(("dp", "fsdp"), None),
            P(("dp", "fsdp"), None),
            P(("dp", "fsdp"), None),
            P(("dp", "fsdp"), None),
            P(("dp", "fsdp"), None),
            P(("dp", "fsdp"), None),
            P(None, ("dp", "fsdp")),
            P(None, ("dp", "fsdp")),
            P(None, ("dp", "fsdp")),
            P(),
        ),
        check_vma=False,
    )
```

profile of v0, /device:TPU:0, one launch (start us, length us, event | category | flops | bytes accessed | tf_op | source)
XLA Modules:
  0.0 992.1 jit_solution(4459537473923290735)
XLA Ops:
  13.9 43.3 %all-gather = bf16[32,24,4]{1,2,0:T(4,128)(2,1)S(1)} all-gather(bf16[1,24,4]{1,2,0:T(4,128)(2,1)S(1)} %convert_bitcast_fusion.2), channel_id=1, replica_groups=mesh['dp'=8,'fsdp'=4] {'dp','fsdp'}, dimensions={0}, use_global_device_ids=true | all-gather | bytes 6336 | tf_op jit(solution)/shard_map/all_gather | solution.py:93
  57.5 3.2 convert_reduce_fusion
  60.7 40.4 %all_gather.20 = bf16[256,512]{1,0:T(8,128)(2,1)} all-gather(bf16[8,512]{1,0:T(8,128)(2,1)S(1)} %convert_element_type.123), channel_id=1, replica_groups=mesh['dp'=8,'fsdp'=4] {'dp','fsdp'}, dimensions={0}, use_global_device_ids=true | all-gather | bytes 270336 | tf_op jit(solution)/shard_map/all_gather | solution.py:92
  101.4 8.2 copy.211
  109.6 6.1 convert_bitcast_fusion
  119.0 6.5 reshape.156
  125.5 8.6 copy.196
  134.2 3.4 fusion.26
  137.7 2.7 select_reduce_fusion
  140.4 2.7 fusion.6
  143.1 2.5 copy-done
  145.6 3.8 fusion.25
  151.5 2.5 slice.73
  156.8 35.5 %multiply_convert_fusion.1 = (bf16[1024,3072]{1,0:T(8,128)(2,1)}, f32[1024,3072]{1,0:T(8,128)}, f32[1024,3072]{1,0:T(8,128)}) fusion(bf16[768,3072]{1,0:T(8,128)(2,1)} %all-gather.7.cloned.1.call-done, f32[1024,768]{1,0:T(8,128)S(1)} %get-tuple-element.172, f32[768]{0:T(1024)S(1)} %get-tuple-element.133, f32[768]{0:T(1024)S(1)} %get-tuple-element.134, ...), kind=kOutput, calls=%fused_computation.6 | convolution fusion | flops 5040242688 | bytes 39335936 | tf_op jit(solution)/shard_map/dot_general | solution.py:138
  192.3 18.4 %all-gather.9.cloned.1.call-done = bf16[3072,768]{1,0:T(8,128)(2,1)} async-done(((bf16[96,768]{1,0:T(8,128)(2,1)}), bf16[3072,768]{1,0:T(8,128)(2,1)}) %all-gather.9.cloned.1.call-update) | async-done | bytes 4718608 | tf_op jit(solution)/shard_map/all_gather | solution.py:97
  210.7 9.2 fusion.82
  222.6 2.9 fusion.15
  225.5 17.8 %add_convert_fusion = bf16[1024,3072]{1,0:T(8,128)(2,1)} fusion(f32[1024,3072]{1,0:T(8,128)} %get-tuple-element.158, f32[1024,3072]{1,0:T(8,128)} %get-tuple-element.173, bf16[3072,768]{1,0:T(8,128)(2,1)} %all-gather.9.cloned.1.call-done, f32[1024,768]{1,0:T(8,128)} %get-tuple-element.159), kind=kOutput, calls=%fused_computation.5 | convolution fusion | flops 4876664832 | bytes 39321600 | tf_op jit(solution)/shard_map/td,fd->tf/dot_general | solution.py:152
  243.3 10.6 %multiply_reduce_fusion.1 = (f32[768]{0:T(1024)}, f32[1024]{0:T(1024)S(1)}, f32[1024]{0:T(1024)S(1)}, f32[768]{0:T(1024)S(1)}, f32[1024,768]{1,0:T(8,128)S(1)}) fusion(f32[1024,768]{1,0:T(8,128)S(1)} %get-tuple-element.172, f32[1024]{0:T(1024)S(1)} %add_rsqrt_fusion.1, f32[1024]{0:T(1024)S(1)} %broadcast_multiply_fusion.4, f32[768]{0:T(1024)S(1)} %get-tuple-element.134, ...), kind=kOutput, calls=%fused_computation.43 | convolution fusion | flops 4839698432 | bytes 20472832 | tf_op jit(solution)/shard_map/tf,df->td/dot_general | solution.py:157
  255.5 2.6 convolution_convert_fusion.1
  258.1 2.9 convolution_bitcast_fusion
  261.1 2.6 copy.176
  263.7 3.8 reshape.159
  267.6 9.1 fusion.28
  276.7 9.6 multiply_reduce_fusion
  286.4 7.5 multiply_convert_fusion
  293.9 2.9 multiply_convert_fusion.3
  296.8 2.4 fusion.27
  299.2 2.3 copy.185
  301.5 2.3 copy.184
  303.8 4.3 fusion.37
  308.1 4.3 convert_bitcast_fusion.1
  312.4 2.8 copy.179
  315.1 3.8 reshape.160
  319.0 2.6 copy.188
  321.7 2.2 copy.187
  324.5 4.1 fusion.21
  328.6 4.3 pad_maximum_fusion
  332.9 12.3 %copy.192 = f32[4,768,768]{2,0,1:T(4,128)} copy(f32[4,768,768]{1,2,0:T(8,128)} %pad_maximum_fusion) | data formatting | bytes 18874368 | tf_op jit(solution)/shard_map/concatenate | solution.py:226
  345.2 10.7 %fusion.65 = f32[768,3072]{1,0:T(8,128)} fusion(bf16[1024,3072]{1,0:T(8,128)(2,1)} %add_convert_fusion, f32[1024,768]{1,0:T(8,128)S(1)} %get-tuple-element.172, f32[768]{0:T(1024)S(1)} %get-tuple-element.133, f32[768]{0:T(1024)S(1)} %get-tuple-element.134, f32[1024]{0:T(1024)S(1)} %add_rsqrt_fusion.1, f32[1024]{0:T(1024)S(1)} %broadcast_multiply_fusion.4), kind=kOutput, calls=%fused_computation.162 | convolution fusion | flops 4835770368 | bytes 18888704 | tf_op jit(solution)/shard_map/td,tf->df/dot_general | solution.py:156
  357.9 10.2 %fusion.40 = f32[3072,768]{1,0:T(8,128)} fusion(bf16[1024,3072]{1,0:T(8,128)(2,1)} %get-tuple-element.157, f32[1024,768]{1,0:T(8,128)S(1)} %copy-done.13), kind=kOutput, calls=%fused_computation.85 | convolution fusion | flops 4832624640 | bytes 18874368 | tf_op jit(solution)/shard_map/tf,td->fd/dot_general | solution.py:151
  370.4 8.8 bitcast_add_fusion
  379.2 75.4 %reduce-scatter.9.cloned.1.call-done = f32[8,512]{1,0:T(8,128)} async-done(((f32[256,512]{1,0:T(8,128)}), f32[8,512]{1,0:T(8,128)}) %reduce-scatter.9.cloned.1.call-update) | async-done | bytes 16400 | tf_op jit(solution)/shard_map/reduce_scatter | solution.py:232
  456.0 192.0 %all-reduce.5.cloned.1.call-done = f32[4,768,768]{2,0,1:T(4,128)} async-done(((f32[4,768,768]{2,0,1:T(4,128)}), f32[4,768,768]{2,0,1:T(4,128)}) %all-reduce.5.cloned.1.call-update) | async-done | bytes 9437200
  651.2 138.3 %reduce-scatter.5.cloned.1.call-done = f32[24,3072]{1,0:T(8,128)} async-done(((f32[768,3072]{1,0:T(8,128)}), f32[24,3072]{1,0:T(8,128)}) %reduce-scatter.5.cloned.1.call-update) | async-done | bytes 294928 | tf_op jit(solution)/shard_map/reduce_scatter | solution.py:229
  789.5 2.1 multiply_reduce_fusion.10
  791.6 139.2 %reduce-scatter.7.cloned.1.call-done = f32[96,768]{1,0:T(8,128)} async-done(((f32[3072,768]{1,0:T(8,128)}), f32[96,768]{1,0:T(8,128)}) %reduce-scatter.7.cloned.1.call-update) | async-done | bytes 294928 | tf_op jit(solution)/shard_map/reduce_scatter | solution.py:230
  937.4 40.1 %all-reduce.2 = (f32[7]{0:T(128)S(1)}, f32[7]{0:T(128)S(1)}, f32[4,768]{1,0:T(4,128)S(1)}) all-reduce(f32[7]{0:T(128)S(1)} %pad_maximum_fusion.14, f32[7]{0:T(128)S(1)} %pad_maximum_fusion.13, f32[4,768]{1,0:T(4,128)S(1)} %copy-done.38), channel_id=1, replica_groups=mesh['dp'=8,'fsdp'=4] {'dp','fsdp'}, use_global_device_ids=true, to_apply=%region_25.26 | all-reduce | flops 3086 | bytes 24688 | tf_op jit(solution)/shard_map/psum | solution.py:247
  (179 shorter events, 41.1 us)
Async XLA Ops:
  7.2 93.9 %copy-start.41 = (s32[2,256]{1,0:T(2,128)S(1)}, s32[2,256]{1,0:T(2,128)}, u32[]{:S(2)}) copy-start(s32[2,256]{1,0:T(2,128)} %param.21) | copy-start | bytes 6148
  7.2 93.9 %copy-start.39 = (s32[2,512]{1,0:T(2,128)S(1)}, s32[2,512]{1,0:T(2,128)}, u32[]{:S(2)}) copy-start(s32[2,512]{1,0:T(2,128)} %param.20) | copy-start | bytes 12292
  7.2 94.1 %all-gather.5.cloned.1.call-start = ((), (), s32[]{:S(2)}) async-start(), calls=%async_computation.3 | async-start | bytes 4866048 | tf_op jit(solution)/shard_map/all_gather | solution.py:91
  9.0 147.8 %all-gather.7.cloned.1.call-start = ((), (), s32[]{:S(2)}) async-start(), calls=%async_computation.4 | async-start | bytes 4866048 | tf_op jit(solution)/shard_map/all_gather | solution.py:96
  10.7 200.0 %all-gather.9.cloned.1.call-start = ((), (), s32[]{:S(2)}) async-start(), calls=%async_computation.5 | async-start | bytes 4866048 | tf_op jit(solution)/shard_map/all_gather | solution.py:97
  12.5 442.2 %reduce-scatter.9.cloned.1.call-start = ((), (), s32[]{:S(2)}) async-start(), calls=%async_computation.8 | async-start | bytes 540672 | tf_op jit(solution)/shard_map/reduce_scatter | solution.py:232
  101.3 41.7 %copy-start.6 = (pred[2,512,256]{1,2,0:T(8,128)(4,1)}, pred[2,512,256]{1,2,0:T(8,128)(4,1)S(1)}, u32[]{:S(2)}) copy-start(pred[2,512,256]{1,2,0:T(8,128)(4,1)S(1)} %broadcast_compare_fusion) | copy-start | bytes 786436
  101.3 8.2 copy-start.47
  119.0 18.7 %copy-start.1 = (bf16[2,512,12,64]{1,0,3,2:T(2,128)(2,1)}, bf16[2,512,12,64]{1,0,3,2:T(2,128)(2,1)S(1)}, u32[]{:S(2)}) copy-start(bf16[2,512,12,64]{1,0,3,2:T(2,128)(2,1)S(1)} %reshape_squeeze.10) | copy-start | bytes 4718596
  125.5 8.6 copy-start.20
  137.7 5.4 copy-start.14
  140.4 5.3 copy-start
  143.0 8.4 slice-start.3
  145.6 5.8 slice-start.4
  151.5 4.2 copy-start.25
  261.1 6.5 copy-start.7
  261.1 6.5 copy-start.32
  267.6 9.1 copy-start.9
  267.6 9.1 copy-start.15
  267.6 18.8 %slice-start = ((s8[12582912]{0:T(1024)(128)(4,1)}), s8[4194304]{0:T(1024)(128)(4,1)S(1)}, s32[]{:S(2)}) async-start(s8[12582912]{0:T(1024)(128)(4,1)} %bitcast.130), calls=%async_computation.10 | async-start | bytes 8388608
  267.6 18.8 %slice-start.1 = ((s8[12582912]{0:T(1024)(128)(4,1)}), s8[4194304]{0:T(1024)(128)(4,1)S(1)}, s32[]{:S(2)}) async-start(s8[12582912]{0:T(1024)(128)(4,1)} %bitcast.130), calls=%async_computation.11 | async-start | bytes 8388608
  276.7 9.6 slice-start.2
  286.4 7.5 copy-start.2
  296.8 7.0 copy-start.40
  296.8 7.0 copy-start.42
  303.8 4.3 copy-start.21
  308.1 4.3 copy-start.8
  321.6 326.4 %all-reduce.5.cloned.1.call-start = ((), (), s32[]{:S(2)}) async-start(), calls=%async_computation.9 | async-start | bytes 18874368
  323.9 4.7 copy-start.11
  345.2 444.3 %reduce-scatter.5.cloned.1.call-start = ((), (), s32[]{:S(2)}) async-start(), calls=%async_computation.6 | async-start | bytes 9732096 | tf_op jit(solution)/shard_map/reduce_scatter | solution.py:229
  356.0 574.8 %reduce-scatter.7.cloned.1.call-start = ((), (), s32[]{:S(2)}) async-start(), calls=%async_computation.7 | async-start | bytes 9732096 | tf_op jit(solution)/shard_map/reduce_scatter | solution.py:230
  370.4 84.2 %copy-start.35 = (f32[8,512]{1,0:T(8,128)S(1)}, f32[8,512]{1,0:T(8,128)}, u32[]{:S(2)}) copy-start(f32[8,512]{1,0:T(8,128)} %param.32) | copy-start | bytes 49156
  379.2 551.6 %copy-start.17 = (f32[96,768]{1,0:T(8,128)S(1)}, f32[96,768]{1,0:T(8,128)}, u32[]{:S(2)}) copy-start(f32[96,768]{1,0:T(8,128)} %param.29) | copy-start | bytes 884740
  379.2 551.6 %copy-start.33 = (f32[96,768]{1,0:T(8,128)S(1)}, f32[96,768]{1,0:T(8,128)}, u32[]{:S(2)}) copy-start(f32[96,768]{1,0:T(8,128)} %param.30) | copy-start | bytes 884740
  379.2 551.6 %copy-start.34 = (f32[96,768]{1,0:T(8,128)S(1)}, f32[96,768]{1,0:T(8,128)}, u32[]{:S(2)}) copy-start(f32[96,768]{1,0:T(8,128)} %param.31) | copy-start | bytes 884740
  379.2 558.2 %copy-start.38 = (f32[4,768]{1,0:T(4,128)S(1)}, f32[4,768]{1,0:T(4,128)}, u32[]{:S(2)}) copy-start(f32[4,768]{1,0:T(4,128)} %pad_maximum_fusion.11) | copy-start | bytes 36868
  379.2 601.4 %copy-start.16 = (f32[4,24,768]{2,1,0:T(8,128)S(1)}, f32[4,24,768]{2,1,0:T(8,128)}, u32[]{:S(2)}) copy-start(f32[4,24,768]{2,1,0:T(8,128)} %param.23) | copy-start | bytes 884740
  456.0 526.3 %copy-start.36 = (f32[8,512]{1,0:T(8,128)}, f32[8,512]{1,0:T(8,128)S(1)}, u32[]{:S(2)}) copy-start(f32[8,512]{1,0:T(8,128)S(1)} %get-tuple-element.155) | copy-start | bytes 49156
  456.0 526.3 %copy-start.37 = (f32[8,512]{1,0:T(8,128)}, f32[8,512]{1,0:T(8,128)S(1)}, u32[]{:S(2)}) copy-start(f32[8,512]{1,0:T(8,128)S(1)} %get-tuple-element.156) | copy-start | bytes 49156
  649.0 332.6 %copy-start.44 = (f32[4,24]{1,0:T(4,128)S(1)}, f32[4,24]{1,0:T(4,128)}, u32[]{:S(2)}) copy-start(f32[4,24]{1,0:T(4,128)} %param.35) | copy-start | bytes 1156
  649.0 332.5 %copy-start.45 = (f32[4,24]{1,0:T(4,128)S(1)}, f32[4,24]{1,0:T(4,128)}, u32[]{:S(2)}) copy-start(f32[4,24]{1,0:T(4,128)} %param.37) | copy-start | bytes 1156
  649.0 332.5 %copy-start.46 = (f32[4,24]{1,0:T(4,128)S(1)}, f32[4,24]{1,0:T(4,128)}, u32[]{:S(2)}) copy-start(f32[4,24]{1,0:T(4,128)} %param.36) | copy-start | bytes 1156
  650.6 334.2 %copy-start.27 = (f32[4,24,768]{2,1,0:T(8,128)}, f32[4,24,768]{2,1,0:T(8,128)S(1)}, u32[]{:S(2)}) copy-start(f32[4,24,768]{2,1,0:T(8,128)S(1)} %get-tuple-element.150) | copy-start | bytes 884740
  650.6 333.3 %copy-start.18 = (f32[24,3072]{1,0:T(8,128)S(1)}, f32[24,3072]{1,0:T(8,128)}, u32[]{:S(2)}) copy-start(f32[24,3072]{1,0:T(8,128)} %param.26) | copy-start | bytes 884740
  791.6 193.2 %copy-start.28 = (f32[24,3072]{1,0:T(8,128)}, f32[24,3072]{1,0:T(8,128)S(1)}, u32[]{:S(2)}) copy-start(f32[24,3072]{1,0:T(8,128)S(1)} %get-tuple-element.151) | copy-start | bytes 884740
  791.6 193.2 %copy-start.29 = (f32[24,3072]{1,0:T(8,128)}, f32[24,3072]{1,0:T(8,128)S(1)}, u32[]{:S(2)}) copy-start(f32[24,3072]{1,0:T(8,128)S(1)} %get-tuple-element.152) | copy-start | bytes 884740
  932.6 52.1 %copy-start.30 = (f32[96,768]{1,0:T(8,128)}, f32[96,768]{1,0:T(8,128)S(1)}, u32[]{:S(2)}) copy-start(f32[96,768]{1,0:T(8,128)S(1)} %get-tuple-element.153) | copy-start | bytes 884740
  932.6 52.1 %copy-start.31 = (f32[96,768]{1,0:T(8,128)}, f32[96,768]{1,0:T(8,128)S(1)}, u32[]{:S(2)}) copy-start(f32[96,768]{1,0:T(8,128)S(1)} %get-tuple-element.154) | copy-start | bytes 884740
  (14 other events, 32.8 us)
Sparse Core Ops, SparseCore 0:
  11.5 67.5 all-gather.4
  82.6 62.1 all-gather.6
  148.2 62.4 all-gather.8
  321.7 132.8 reduce-scatter.8
  461.2 186.7 all-reduce.4
  653.8 135.6 reduce-scatter.4
  796.4 134.3 reduce-scatter.6
where the time goes:
time: 1000 us; the launch traced here: 992 us
  waiting for transfers between devices  563 us (56%)
  matrix products  162 us (16%)
  blocking collectives  124 us (12%)
  local copies, waits for them, and re-layouts  79.2 us (8%)
  other arithmetic  45.7 us (5%)
  between operations  17.2 us (2%)
    unnamed x8, waiting for transfers between devices  192 us
    reduce_scatter x1, waiting for transfers between devices, local(): lax.psum_scatter(down_grad, ('dp', 'fsdp'), scatter_dimension=0, tiled=True)  139 us
    reduce_scatter x1, waiting for transfers between devices, local(): lax.psum_scatter(up_grad, ('dp', 'fsdp'), scatter_dimension=0, tiled=True)  138 us
    reduce_scatter x1, waiting for transfers between devices, local(): lax.psum_scatter(comp_grad, ('dp', 'fsdp'), scatter_dimension=0, tiled=True)  75.4 us
    all_gather x1, blocking collectives, local(): lax.all_gather(norm_params.astype(low_type), ('dp', 'fsdp'), axis=1, tile...  43.3 us
    all_gather x1, blocking collectives, local(): lax.all_gather(compress_weight.astype(low_type), ('dp', 'fsdp'), axis=0,...  40.4 us
    psum x1, blocking collectives, local(): lax.psum((matrix_squares(attn_weight, up_weight, down_weight, compress_we...  40.1 us
    dot_general x1, matrix products, local(): hidden = jnp.dot(first_low, up_full, preferred_element_type=full_type)  35.5 us
  transfers between devices with their start and end apart: 7, of which 5 were waited for; matrix products, arithmetic and copies ran while one was open for 16% of the time, Pallas kernels for 0%

commit v1 on v0

--- a/solution.py
+++ b/solution.py
@@ -14,6 +14,90 @@
 RATE = 0.5
 NORM_EPS = 1e-05
 MASKED = -1e30
+
+AXES = ("dp", "fsdp")
+LOW = jnp.bfloat16
+FULL = jnp.float32
+
+
+class Exchange:
+    def __init__(self, dp, fsdp):
+        self.count = dp * fsdp
+        self.bits = self.count.bit_length() - 1
+        self.x_bit = 1
+        self.y_bit = fsdp.bit_length() - 1
+        self.rest = [b for b in range(1, self.bits) if b not in (self.x_bit, self.y_bit)]
+        index = lax.axis_index(AXES)
+        self.values = [(index >> b) & 1 for b in range(self.bits)]
+        self.core = self.values[0]
+
+    def flip(self, array, even_bit, odd_bit):
+        pairs = [(i, i ^ (1 << (odd_bit if i & 1 else even_bit))) for i in range(self.count)]
+        return lax.ppermute(array, AXES, pairs)
+
+    def by_core(self, even, odd):
+        return jnp.where(self.core == 0, even, odd)
+
+    def joined(self, own, other, value, axis):
+        return jnp.where(
+            value == 0, jnp.stack([own, other], axis), jnp.stack([other, own], axis)
+        )
+
+    def gather(self, shard):
+        have = shard
+        for place, bit in enumerate(reversed(self.rest)):
+            have = self.joined(have, self.flip(have, bit, bit), self.values[bit], place)
+        x_value, y_value = self.values[self.x_bit], self.values[self.y_bit]
+        got = self.flip(have, self.y_bit, self.x_bit)
+        have = self.joined(have, got, self.by_core(y_value, x_value), 0)
+        got = self.flip(have, self.x_bit, self.y_bit)
+        have = self.joined(have, got, self.by_core(x_value, y_value), 0)
+        got = self.flip(have, 0, 0)
+        even, odd = self.by_core(have, got), self.by_core(got, have)
+        now_even = [self.x_bit, self.y_bit] + self.rest[::-1]
+        now_odd = [self.y_bit, self.x_bit] + self.rest[::-1]
+        wanted = list(range(self.bits - 1, 0, -1))
+        tail = [len(wanted), len(wanted) + 1]
+        even = even.transpose([now_even.index(b) for b in wanted] + tail)
+        odd = odd.transpose([now_odd.index(b) for b in wanted] + tail)
+        whole = jnp.stack([even, odd], axis=len(wanted))
+        return whole.reshape((self.count,) + shard.shape)
+
+    def scatter(self, blocks):
+        shape = blocks.shape[1:]
+        view = blocks.reshape((2,) * self.bits + shape)
+
+        def pick(array, dim, value):
+            return lax.dynamic_index_in_dim(array, value, dim, keepdims=False)
+
+        dim = self.bits - 1
+        got = self.flip(pick(view, dim, 1 - self.core).astype(LOW), 0, 0)
+        view = (pick(view, dim, self.core).astype(FULL) + got.astype(FULL)).astype(LOW)
+        bits = list(range(self.bits - 1, 0, -1))
+        dim_x, dim_y = bits.index(self.x_bit), bits.index(self.y_bit)
+        x_value, y_value = self.values[self.x_bit], self.values[self.y_bit]
+
+        def halves(x_now, y_now):
+            even = pick(jnp.moveaxis(view, (dim_x, dim_y), (0, 1)), 0, x_now)
+            odd = pick(jnp.moveaxis(view, (dim_y, dim_x), (0, 1)), 0, y_now)
+            return self.by_core(even, odd)
+
+        got = self.flip(halves(1 - x_value, 1 - y_value), self.x_bit, self.y_bit)
+        view = halves(x_value, y_value).astype(FULL) + got.astype(FULL)
+        value = self.by_core(y_value, x_value)
+        got = self.flip(pick(view, 0, 1 - value).astype(LOW), self.y_bit, self.x_bit)
+        view = pick(view, 0, value) + got.astype(FULL)
+        for dim, bit in reversed(list(enumerate(self.rest[::-1]))):
+            value = self.values[bit]
+            got = self.flip(pick(view, dim, 1 - value).astype(LOW), bit, bit)
+            view = pick(view, dim, value) + got.astype(FULL)
+        return view
+
+    def total(self, vector):
+        row = jnp.zeros((8, 128), FULL).at[0, : vector.shape[0]].set(vector)
+        sent = jnp.broadcast_to(row[None], (self.count, 8, 128))
+        got = lax.all_to_all(sent, AXES, split_axis=0, concat_axis=0, tiled=True)
+        return jnp.sum(got, axis=0)[0, : vector.shape[0]]
 
 
 def gelu_exact(argument):
@@ -65,6 +149,8 @@
 
 
 def local(
+    dp,
+    fsdp,
     inputs,
     segment_ids,
     compressed_segment,
@@ -85,19 +171,46 @@
     norm_first,
     norm_second,
 ):
-    low_type = jnp.bfloat16
-    full_type = jnp.float32
-    attn_full, compress_full, norm_full = (
-        lax.all_gather(attn_weight.astype(low_type), ("dp", "fsdp"), axis=1, tiled=True),
-        lax.all_gather(compress_weight.astype(low_type), ("dp", "fsdp"), axis=0, tiled=True),
-        lax.all_gather(norm_params.astype(low_type), ("dp", "fsdp"), axis=1, tiled=True),
-    )
-    up_full, down_full = (
-        lax.all_gather(up_weight.astype(low_type), ("dp", "fsdp"), axis=0, tiled=True),
-        lax.all_gather(down_weight.astype(low_type), ("dp", "fsdp"), axis=0, tiled=True),
+    low_type = LOW
+    full_type = FULL
+    exchange = Exchange(dp, fsdp)
+    devices = dp * fsdp
+    row_count, length, model_width = inputs.shape
+    norm_kinds, norm_own = norm_params.shape
+    attn_kinds, attn_own, _ = attn_weight.shape
+    compress_own = compress_weight.shape[0]
+    spare = model_width - length
+    side_rows = max(compress_own, norm_kinds)
+
+    def side_block(compress_part, norm_part):
+        none = [(0, 0)] * (compress_part.ndim - 2)
+        left = jnp.pad(compress_part, none + [(0, side_rows - compress_own), (0, 0)])
+        right = jnp.pad(norm_part, none + [(0, side_rows - norm_kinds), (0, spare - norm_own)])
+        return jnp.concatenate([left, right], axis=-1)
+
+    attn_pack = jnp.concatenate(
+        [
+            attn_weight.astype(low_type).reshape(attn_kinds * attn_own, model_width),
+            side_block(compress_weight.astype(low_type), norm_params.astype(low_type)),
+        ]
+    )
+    attn_blocks = exchange.gather(attn_pack)
+    up_full = exchange.gather(up_weight.astype(low_type)).reshape(model_width, -1)
+    down_full = exchange.gather(down_weight.astype(low_type)).reshape(-1, model_width)
+    attn_full = (
+        attn_blocks[:, : attn_kinds * attn_own]
+        .reshape(devices, attn_kinds, attn_own, model_width)
+        .transpose(1, 0, 2, 3)
+        .reshape(attn_kinds, model_width, model_width)
+    )
+    side = attn_blocks[:, attn_kinds * attn_own :]
+    compress_full = side[:, :compress_own, :length].reshape(-1, length)
+    norm_full = (
+        side[:, :norm_kinds, length : length + norm_own]
+        .transpose(1, 0, 2)
+        .reshape(norm_kinds, model_width)
     )
     gains = norm_full.astype(full_type)
-    row_count, length, model_width = inputs.shape
     head_count = model_width // HEAD_DIM
     token_count = row_count * length
     score_scale = HEAD_DIM ** (-0.5)
@@ -141,36 +254,33 @@
     branch = jnp.dot(active, down_full, preferred_element_type=full_type)
     second_out, second_normed, second_inv = norm_forward(first_out + branch, gains[2], gains[3])
     result = second_out.astype(low_type).reshape(row_count, length, model_width)
-    up_back, down_back = (
-        lax.all_gather(up_weight.astype(low_type), ("dp", "fsdp"), axis=0, tiled=True),
-        lax.all_gather(down_weight.astype(low_type), ("dp", "fsdp"), axis=0, tiled=True),
-    )
     grad_top = out_grad.reshape(token_count, model_width).astype(full_type)
     grad_second, gain_two, bias_two = norm_backward(grad_top, second_normed, second_inv, gains[2])
     grad_second_low = grad_second.astype(low_type)
-    down_grad = jnp.einsum("tf,td->fd", active, grad_second_low, preferred_element_type=full_type)
+    down_grad = jnp.einsum(
+        "tf,td->fd", active, grad_second_low, preferred_element_type=full_type
+    ).astype(low_type)
+    down_owned = exchange.scatter(down_grad.reshape((devices,) + down_weight.shape))
     grad_active = jnp.einsum(
-        "td,fd->tf", grad_second_low, down_back, preferred_element_type=full_type
+        "td,fd->tf", grad_second_low, down_full, preferred_element_type=full_type
     )
     grad_hidden_low = gelu_pull(grad_active)[0].astype(low_type)
-    up_grad = jnp.einsum("td,tf->df", first_low, grad_hidden_low, preferred_element_type=full_type)
+    up_grad = jnp.einsum(
+        "td,tf->df", first_low, grad_hidden_low, preferred_element_type=full_type
+    ).astype(low_type)
+    up_owned = exchange.scatter(up_grad.reshape((devices,) + up_weight.shape))
     grad_first_out = grad_second + jnp.einsum(
-        "tf,df->td", grad_hidden_low, up_back, preferred_element_type=full_type
-    )
-    attn_back, compress_back = (
-        lax.all_gather(attn_weight.astype(low_type), ("dp", "fsdp"), axis=1, tiled=True),
-        lax.all_gather(compress_weight.astype(low_type), ("dp", "fsdp"), axis=0, tiled=True),
-    )
-    masked_back = jnp.where(member, compress_back[None], jnp.zeros((), low_type))
+        "tf,df->td", grad_hidden_low, up_full, preferred_element_type=full_type
+    )
     grad_first, gain_one, bias_one = norm_backward(
         grad_first_out, first_normed, first_inv, gains[0]
     )
     grad_first_low = grad_first.astype(low_type)
     out_proj_grad = jnp.einsum(
         "td,te->de", context, grad_first_low, preferred_element_type=full_type
-    )
+    ).astype(low_type)
     grad_context = (
-        jnp.einsum("te,de->td", grad_first_low, attn_back[3], preferred_element_type=full_type)
+        jnp.einsum("te,de->td", grad_first_low, attn_full[3], preferred_element_type=full_type)
         .astype(low_type)
         .reshape(row_count, length, head_count, HEAD_DIM)
     )
@@ -203,7 +313,7 @@
         ]
     )
     grad_kv = jnp.einsum(
-        "rks,jrkd->jrsd", masked_back, grad_comp, preferred_element_type=full_type
+        "rks,jrkd->jrsd", masked_proj, grad_comp, preferred_element_type=full_type
     ).astype(low_type)
     comp_grad = jnp.sum(
         jnp.where(
@@ -219,19 +329,30 @@
             grad_kv.reshape(2, token_count, model_width),
         ]
     )
-    qkv_grad = jnp.einsum("td,jte->jde", flat_in, grad_qkv, preferred_element_type=full_type)
+    qkv_grad = jnp.einsum(
+        "td,jte->jde", flat_in, grad_qkv, preferred_element_type=full_type
+    ).astype(low_type)
     input_grad = grad_first + jnp.einsum(
-        "jte,jde->td", grad_qkv, attn_back[:3], preferred_element_type=full_type
+        "jte,jde->td", grad_qkv, attn_full[:3], preferred_element_type=full_type
     )
     attn_grad = jnp.concatenate([qkv_grad, out_proj_grad[None]])
     norm_grad = jnp.stack([gain_one, bias_one, gain_two, bias_two])
-    up_owned, down_owned, attn_owned, compress_owned, norm_owned = (
-        lax.psum_scatter(up_grad, ("dp", "fsdp"), scatter_dimension=0, tiled=True),
-        lax.psum_scatter(down_grad, ("dp", "fsdp"), scatter_dimension=0, tiled=True),
-        lax.psum_scatter(attn_grad, ("dp", "fsdp"), scatter_dimension=1, tiled=True),
-        lax.psum_scatter(comp_grad, ("dp", "fsdp"), scatter_dimension=0, tiled=True),
-        lax.psum_scatter(norm_grad, ("dp", "fsdp"), scatter_dimension=1, tiled=True),
-    )
+    grad_pack = jnp.concatenate(
+        [
+            attn_grad.reshape(attn_kinds, devices, attn_own, model_width)
+            .transpose(1, 0, 2, 3)
+            .reshape(devices, attn_kinds * attn_own, model_width),
+            side_block(
+                comp_grad.reshape(devices, compress_own, length),
+                norm_grad.reshape(norm_kinds, devices, norm_own).transpose(1, 0, 2),
+            ).astype(low_type),
+        ],
+        axis=1,
+    )
+    owned = exchange.scatter(grad_pack)
+    attn_owned = owned[: attn_kinds * attn_own].reshape(attn_weight.shape)
+    compress_owned = owned[attn_kinds * attn_own :, :length][:compress_own]
+    norm_owned = owned[attn_kinds * attn_own :, length:][:norm_kinds, :norm_own]
     attn_first_new, attn_second_new, attn_direction = adaptive(attn_first, attn_second, attn_owned)
     up_first_new, up_second_new, up_direction = adaptive(up_first, up_second, up_owned)
     down_first_new, down_second_new, down_direction = adaptive(down_first, down_second, down_owned)
@@ -243,13 +364,15 @@
     up_direction = up_direction + DECAY * up_weight
     down_direction = down_direction + DECAY * down_weight
     compress_direction = compress_direction + DECAY * compress_weight
-    update_sq = matrix_squares(attn_direction, up_direction, down_direction, compress_direction)
-    weight_sq, update_total = lax.psum(
-        (matrix_squares(attn_weight, up_weight, down_weight, compress_weight), update_sq),
-        ("dp", "fsdp"),
-    )
-    weight_norm = jnp.sqrt(weight_sq)
-    update_norm = jnp.sqrt(update_total)
+    squares = exchange.total(
+        jnp.concatenate(
+            [
+                matrix_squares(attn_weight, up_weight, down_weight, compress_weight),
+                matrix_squares(attn_direction, up_direction, down_direction, compress_direction),
+            ]
+        )
+    )
+    weight_norm, update_norm = jnp.sqrt(squares[:7]), jnp.sqrt(squares[7:])
     trust_ratio = weight_norm / (update_norm + EPSILON)
     attn_new = attn_weight - RATE * trust_ratio[:4].reshape(4, 1, 1) * attn_direction
     up_new = up_weight - RATE * trust_ratio[4] * up_direction
@@ -285,54 +408,19 @@
 
 
 def solution(mesh):
+    rows, mid, flat = P(AXES, None), P(None, AXES, None), P(None, AXES)
+    deep = P(AXES, None, None)
+
+    def step(*args):
+        return local(mesh.shape["dp"], mesh.shape["fsdp"], *args)
+
     return jax.shard_map(
-        local,
+        step,
         mesh=mesh,
-        in_specs=(
-            P(("dp", "fsdp"), None, None),
-            P(("dp", "fsdp"), None),
-            P(("dp", "fsdp"), None),
-            P(("dp", "fsdp"), None, None),
-            P(None, ("dp", "fsdp"), None),
-            P(None, ("dp", "fsdp"), None),
-            P(None, ("dp", "fsdp"), None),
-            P(("dp", "fsdp"), None),
-            P(("dp", "fsdp"), None),
-            P(("dp", "fsdp"), None),
-            P(("dp", "fsdp"), None),
-            P(("dp", "fsdp"), None),
-            P(("dp", "fsdp"), None),
-            P(("dp", "fsdp"), None),
-            P(("dp", "fsdp"), None),
-            P(("dp", "fsdp"), None),
-            P(None, ("dp", "fsdp")),
-            P(None, ("dp", "fsdp")),
-            P(None, ("dp", "fsdp")),
-        ),
-        out_specs=(
-            P(("dp", "fsdp"), None, None),
-            P(("dp", "fsdp"), None, None),
-            P(None, ("dp", "fsdp"), None),
-            P(None, ("dp", "fsdp"), None),
-            P(("dp", "fsdp"), None),
-            P(None, ("dp", "fsdp"), None),
-            P(None, ("dp", "fsdp"), None),
-            P(("dp", "fsdp"), None),
-            P(("dp", "fsdp"), None),
-            P(("dp", "fsdp"), None),
-            P(("dp", "fsdp"), None),
-            P(("dp", "fsdp"), None),
-            P(("dp", "fsdp"), None),
-            P(("dp", "fsdp"), None),
-            P(("dp", "fsdp"), None),
-            P(("dp", "fsdp"), None),
-            P(("dp", "fsdp"), None),
-            P(("dp", "fsdp"), None),
-            P(("dp", "fsdp"), None),
-            P(None, ("dp", "fsdp")),
-            P(None, ("dp", "fsdp")),
-            P(None, ("dp", "fsdp")),
-            P(),
-        ),
+        in_specs=(deep, rows, rows, deep) + (mid,) * 3 + (rows,) * 9 + (flat,) * 3,
+        out_specs=(deep, deep, mid, mid, rows, mid, mid)
+        + (rows,) * 12
+        + (flat,) * 3
+        + (P(),),
         check_vma=False,
     )

time: 1000 us -> 464 us (0.46)
  waiting for transfers between devices: 563 us -> 115 us
  blocking collectives: 124 us -> 0 us
  starting transfers between devices: 0.29 us -> 53.3 us
  other arithmetic: 45.7 us -> 71.8 us
  local copies, waits for them, and re-layouts: 79.2 us -> 62.4 us
  between operations: 17.2 us -> 4.74 us
  matrix products: 162 us -> 151 us
    reduce_scatter x3 -> x0, waiting for transfers between devices: 353 us -> none  [the longest x1 139 us: local(): lax.psum_scatter(down_grad, ('dp', 'fsdp'), scatter_dimension=0, tiled=True)]
    unnamed x8 -> x0, waiting for transfers between devices: 192 us -> none
    ppermute x0 -> x30, waiting for transfers between devices: none -> 109 us  [flip(): return lax.ppermute(array, AXES, pairs)]
    all_gather x2 -> x0, blocking collectives: 83.6 us -> none  [the longest x1 43.3 us: local(): lax.all_gather(norm_params.astype(low_type), ('dp', 'fsdp'), axis=1, tile...]
    ppermute x0 -> x30, starting transfers between devices: none -> 48.8 us  [flip(): return lax.ppermute(array, AXES, pairs)]
    psum x1 -> x0, blocking collectives: 40.1 us -> none  [local(): lax.psum((matrix_squares(attn_weight, up_weight, down_weight, compress_we...]
    all_gather x3 -> x0, waiting for transfers between devices: 18.4 us -> none  [the longest x1 18.4 us: local(): lax.all_gather(down_weight.astype(low_type), ('dp', 'fsdp'), axis=0, tile...]
    another operation x1 -> x21, other arithmetic: 0.62 us -> 17.5 us  [the longest x6 11.7 us: gather(): whole = jnp.stack([even, odd], axis=len(wanted))]
  transfers between devices with their start and end apart: 7 -> 31, of which waited for: 5 -> 17; matrix products, arithmetic and copies ran while one was open for 16% -> 17% of each run, Pallas kernels for 0% -> 0%
where the time goes in v1:
time: 464 us; the launch traced here: 459 us
  matrix products  151 us (33%)
  waiting for transfers between devices  115 us (25%)
  other arithmetic  71.8 us (15%)
  local copies, waits for them, and re-layouts  62.4 us (13%)
  starting transfers between devices  53.3 us (11%)
  between operations  4.74 us (1%)
    ppermute x30, waiting for transfers between devices, flip(): return lax.ppermute(array, AXES, pairs)  109 us
    ppermute x30, starting transfers between devices, flip(): return lax.ppermute(array, AXES, pairs)  48.8 us
    dot_general x1, matrix products, local(): hidden = jnp.dot(first_low, up_full, preferred_element_type=full_type)  37.3 us
    dot_general x1, matrix products, local(): jnp.einsum('td,fd->tf', grad_second_low, down_full, preferred_element_typ...  18.5 us
    another operation x6, other arithmetic, gather(): whole = jnp.stack([even, odd], axis=len(wanted))  11.7 us
    dot_general x1, matrix products, local(): jnp.einsum('tf,td->fd', active, grad_second_low, preferred_element_type=f...  11.1 us
    dot_general x1, matrix products, local(): branch = jnp.dot(active, down_full, preferred_element_type=full_type)  10.9 us
    reshape x2, local copies, waits for them, and re-layouts, local(): kv_low = projected[1:3].reshape(2, row_count, length, model_width)  10.9 us
  transfers between devices with their start and end apart: 31, of which 17 were waited for; matrix products, arithmetic and copies ran while one was open for 17% of the time, Pallas kernels for 0%

profile of v1, /device:TPU:0, one launch (start us, length us, event | category | flops | bytes accessed | tf_op | source)
XLA Modules:
  0.0 458.7 jit_solution(8477243877422779286)
XLA Ops:
  1.7 4.1 collective-permute-start.10
  9.3 3.0 collective-permute-start.5
  15.3 10.7 %collective-permute-done.5 = bf16[24,3072]{1,0:T(8,128)(2,1)S(1)} collective-permute-done((bf16[24,3072]{1,0:T(8,128)(2,1)S(1)}, bf16[24,3072]{1,0:T(8,128)(2,1)S(1)}, u32[]{:S(2)}, u32[]{:S(2)}) %collective-permute-start.5) | collective-permute-done | bytes 147488 | tf_op jit(solution)/shard_map/ppermute | solution.py:36
  29.3 6.8 %collective-permute-done.11 = bf16[2,96,768]{2,1,0:T(8,128)(2,1)S(1)} collective-permute-done((bf16[2,96,768]{2,1,0:T(8,128)(2,1)S(1)}, bf16[2,96,768]{2,1,0:T(8,128)(2,1)S(1)}, u32[]{:S(2)}, u32[]{:S(2)}) %collective-permute-start.11) | collective-permute-done | bytes 294944 | tf_op jit(solution)/shard_map/ppermute | solution.py:36
  37.8 4.6 %collective-permute-done.6 = bf16[2,24,3072]{2,1,0:T(8,128)(2,1)S(1)} collective-permute-done((bf16[2,24,3072]{2,1,0:T(8,128)(2,1)S(1)}, bf16[2,24,3072]{2,1,0:T(8,128)(2,1)S(1)}, u32[]{:S(2)}, u32[]{:S(2)}) %collective-permute-start.6) | collective-permute-done | bytes 294944 | tf_op jit(solution)/shard_map/ppermute | solution.py:36
  44.5 3.0 collective-permute-done.1
  50.8 4.0 collective-permute-done.7
  57.9 10.2 %collective-permute-done.13 = bf16[2,2,2,96,768]{4,3,0,2,1:T(8,128)(2,1)S(1)} collective-permute-done((bf16[2,2,2,96,768]{4,3,0,2,1:T(8,128)(2,1)S(1)}, bf16[2,2,2,96,768]{4,3,0,2,1:T(8,128)(2,1)S(1)}, u32[]{:S(2)}, u32[]{:S(2)}) %collective-permute-start.13) | collective-permute-done | bytes 1179680 | tf_op jit(solution)/shard_map/ppermute | solution.py:36
  69.8 3.9 collective-permute-start.14
  76.7 4.0 collective-permute-done.8
  83.5 4.0 collective-permute-start.9
  91.0 3.6 collective-permute-done.3
  96.9 3.7 collective-permute-start.4
  102.5 2.6 pad_maximum_fusion.2
  115.9 4.1 convert_bitcast_fusion
  122.8 3.9 reshape.1193
  126.7 7.0 %copy.167 = bf16[2,2,512,768]{3,2,0,1:T(8,128)(2,1)S(1)} copy(bf16[2,2,512,768]{2,1,3,0:T(2,128)(2,1)} %reshape.1193) | data formatting | bytes 6291456 | tf_op jit(solution)/shard_map/reshape | solution.py:222
  137.5 2.9 reshape_squeeze.10
  140.5 3.2 select_reduce_fusion
  143.7 2.7 fusion.6
  148.4 3.5 fusion.28
  156.6 37.3 %multiply_convert_fusion.1 = (bf16[1024,3072]{1,0:T(8,128)(2,1)S(1)}, f32[1024,3072]{1,0:T(8,128)}, f32[1024,3072]{1,0:T(8,128)}) fusion(bf16[768,3072]{1,0:T(8,128)(2,1)} %bitcast.375, f32[1024,768]{1,0:T(8,128)S(1)} %get-tuple-element.109, f32[768]{0:T(1024)S(1)} %add.272, f32[768]{0:T(1024)S(1)} %mul.404, f32[1024]{0:T(1024)S(1)} %add_rsqrt_fusion.1, ...), kind=kOutput, calls=%fused_computation.6 | convolution fusion | flops 5040242688 | bytes 39335936 | tf_op jit(solution)/shard_map/dot_general | solution.py:251
  194.0 10.9 %fusion.103 = (f32[1024]{0:T(1024)S(1)}, f32[1024,768]{1,0:T(8,128)S(1)}) fusion(bf16[1024,3072]{1,0:T(8,128)(2,1)S(1)} %get-tuple-element.72, bf16[3072,768]{1,0:T(8,128)(2,1)} %bitcast.373, f32[768]{0:T(1024)S(1)} %add.272, f32[768]{0:T(1024)S(1)} %mul.404, f32[1024]{0:T(1024)S(1)} %add_rsqrt_fusion.1, f32[1024,768]{1,0:T(8,128)} %copy-done.6, ...), kind=kOutput, calls=%fused_computation.273 | convolution fusion | flops 4836555776 | bytes 17319936 | tf_op jit(solution)/shard_map/dot_general | solution.py:254
  210.0 3.3 fusion.18
  213.3 11.1 %convolution_convert_fusion = bf16[3072,768]{1,0:T(8,128)(2,1)} fusion(bf16[1024,3072]{1,0:T(8,128)(2,1)} %copy-done.76, f32[1024,768]{1,0:T(8,128)S(1)} %get-tuple-element.84), kind=kOutput, calls=%fused_computation.32 | convolution fusion | flops 4834983936 | bytes 14155776 | tf_op jit(solution)/shard_map/tf,td->fd/dot_general | solution.py:260
  224.4 18.5 %add_convert_fusion = bf16[1024,3072]{1,0:T(8,128)(2,1)} fusion(f32[1024,3072]{1,0:T(8,128)} %get-tuple-element.73, f32[1024,3072]{1,0:T(8,128)} %get-tuple-element.110, bf16[3072,768]{1,0:T(8,128)(2,1)} %bitcast.374, f32[1024,768]{1,0:T(8,128)} %copy-done.31), kind=kOutput, calls=%fused_computation.5 | convolution fusion | flops 4876664832 | bytes 39321600 | tf_op jit(solution)/shard_map/td,fd->tf/dot_general | solution.py:264
  242.8 10.0 %convolution_convert_fusion.1 = bf16[768,3072]{1,0:T(8,128)(2,1)} fusion(bf16[1024,3072]{1,0:T(8,128)(2,1)} %add_convert_fusion, f32[1024,768]{1,0:T(8,128)S(1)} %copy-done.7, f32[768]{0:T(1024)S(1)} %add.272, f32[768]{0:T(1024)S(1)} %mul.404, f32[1024]{0:T(1024)S(1)} %add_rsqrt_fusion.1, f32[1024]{0:T(1024)S(1)} %broadcast_multiply_fusion.4), kind=kOutput, calls=%fused_computation.33 | convolution fusion | flops 4838129664 | bytes 14170112 | tf_op jit(solution)/shard_map/td,tf->df/dot_general | solution.py:268
  252.9 8.5 %multiply_reduce_fusion.1 = (bf16[768]{0:T(1024)(128)(2,1)S(1)}, f32[1024]{0:T(1024)S(1)}, f32[1024]{0:T(1024)S(1)}, bf16[768]{0:T(1024)(128)(2,1)S(1)}, f32[1024,768]{1,0:T(8,128)S(1)}) fusion(f32[1024,768]{1,0:T(8,128)S(1)} %copy-done.7, f32[1024]{0:T(1024)S(1)} %add_rsqrt_fusion.1, f32[1024]{0:T(1024)S(1)} %broadcast_multiply_fusion.4, ...), kind=kOutput, calls=%fused_computation.54 | convolution fusion | flops 4839698432 | bytes 20469760 | tf_op jit(solution)/shard_map/tf,df->td/dot_general | solution.py:272
  264.4 2.6 convolution_convert_fusion.3
  271.2 8.5 %multiply_reduce_fusion = (f32[2,12,512]{2,1,0:T(8,128)S(1)}, f32[2,12,512,256]{2,3,1,0:T(8,128)S(1)}) fusion(f32[2,12,512,256]{2,3,1,0:T(8,128)} %copy-done, f32[2,12,512]{2,1,0:T(8,128)S(1)} %log_add_fusion, pred[2,512,256]{1,2,0:T(8,128)(4,1)S(1)} %copy-done.19, bf16[2,256,12,64]{1,3,2,0:T(8,128)(2,1)S(1)} %bitcast.390, ...), kind=kOutput, calls=%fused_computation.3 | convolution fusion | flops 418369536 | bytes 27885568 | tf_op jit(solution)/shard_map/rshe,rkhe->rhsk/dot_general | solution.py:293
  279.7 8.1 %multiply_convert_fusion = bf16[2,12,512,256]{2,3,1,0:T(8,128)(2,1)S(1)} fusion(f32[2,12,512,256]{2,3,1,0:T(8,128)S(1)} %get-tuple-element.115, f32[2,12,512,256]{2,3,1,0:T(8,128)} %copy-done, f32[2,12,512]{2,1,0:T(8,128)S(1)} %get-tuple-element.114, f32[2,12,512]{2,1,0:T(8,128)S(1)} %log_add_fusion, pred[2,512,256]{1,2,0:T(8,128)(4,1)S(1)} %copy-done.19), kind=kLoop, calls=%fused_computation.2 | loop fusion | flops 18874368 | bytes 31817728 | tf_op jit(solution)/shard_map/convert_element_type | solution.py:297
  290.2 2.9 multiply_convert_fusion.3
  293.1 4.2 fusion.31
  311.2 2.7 convert_bitcast_fusion.1
  322.7 3.9 convolution_convert_fusion.4
  326.7 4.5 fusion.26
  339.2 2.7 fusion.14
  344.4 5.5 %bitcast_add_fusion = f32[1024,768]{1,0:T(8,128)} fusion(f32[1024,768]{1,0:T(8,128)S(1)} %copy-done.30, bf16[3,768,768]{2,1,0:T(8,128)(2,1)S(1)} %bitcast.384, bf16[2,1024,768]{2,1,0:T(8,128)(2,1)S(1)} %bitcast.388, bf16[1,1024,768]{2,1,0:T(8,128)(2,1)S(1)} %copy-done.39), kind=kOutput, calls=%fused_computation.43 | convolution fusion | flops 3627024384 | bytes 14548992 | tf_op jit(solution)/shard_map/jte,jde->td/dot_general | solution.py:335
  356.2 16.9 %collective-permute-done.21 = bf16[2,2,2,24,3072]{4,3,1,2,0:T(8,128)(2,1)} collective-permute-done((bf16[2,2,2,24,3072]{4,3,1,2,0:T(8,128)(2,1)}, bf16[2,2,2,24,3072]{4,3,1,2,0:T(8,128)(2,1)}, u32[]{:S(2)}, u32[]{:S(2)}) %collective-permute-start.21) | collective-permute-done | bytes 1179680 | tf_op jit(solution)/shard_map/ppermute | solution.py:36
  376.7 16.4 %collective-permute-done.16 = bf16[2,2,2,104,768]{4,3,0,2,1:T(8,128)(2,1)S(1)} collective-permute-done((bf16[2,2,2,104,768]{4,3,0,2,1:T(8,128)(2,1)S(1)}, bf16[2,2,2,104,768]{4,3,0,2,1:T(8,128)(2,1)S(1)}, u32[]{:S(2)}, u32[]{:S(2)}) %collective-permute-start.16) | collective-permute-done | bytes 1277984 | tf_op jit(solution)/shard_map/ppermute | solution.py:36
  397.7 9.3 %collective-permute-done.28 = bf16[2,96,768]{2,1,0:T(8,128)(2,1)S(1)} collective-permute-done((bf16[2,96,768]{2,1,0:T(8,128)(2,1)S(1)}, bf16[2,96,768]{2,1,0:T(8,128)(2,1)S(1)}, u32[]{:S(2)}, u32[]{:S(2)}) %collective-permute-start.28) | collective-permute-done | bytes 294944 | tf_op jit(solution)/shard_map/ppermute | solution.py:36
  407.5 3.7 collective-permute-done.23
  412.3 3.4 collective-permute-start.24
  417.0 6.5 %collective-permute-done.18 = bf16[2,104,768]{2,1,0:T(8,128)(2,1)S(1)} collective-permute-done((bf16[2,104,768]{2,1,0:T(8,128)(2,1)S(1)}, bf16[2,104,768]{2,1,0:T(8,128)(2,1)S(1)}, u32[]{:S(2)}, u32[]{:S(2)}) %collective-permute-start.18) | collective-permute-done | bytes 319520 | tf_op jit(solution)/shard_map/ppermute | solution.py:36
  426.2 6.7 %collective-permute-done.19 = bf16[104,768]{1,0:T(8,128)(2,1)S(1)} collective-permute-done((bf16[104,768]{1,0:T(8,128)(2,1)S(1)}, bf16[104,768]{1,0:T(8,128)(2,1)S(1)}, u32[]{:S(2)}, u32[]{:S(2)}) %collective-permute-start.19) | collective-permute-done | bytes 159776 | tf_op jit(solution)/shard_map/ppermute | solution.py:36
  434.1 4.0 concatenate.284
  438.7 4.6 all-to-all-start
  445.3 6.3 %all-to-all-done = f32[32,8,128]{2,1,0:T(8,128)S(1)} async-done(((f32[32,8,128]{2,1,0:T(8,128)}), f32[32,8,128]{2,1,0:T(8,128)S(1)}, u32[]{:S(2)}, u32[]{:S(2)}) %all-to-all-start) | async-done | bytes 131104 | tf_op jit(solution)/shard_map/all_to_all | solution.py:99
  (359 shorter events, 135.2 us)
Async XLA Ops:
  1.7 24.4 %collective-permute-start.10 = (bf16[96,768]{1,0:T(8,128)(2,1)S(1)}, bf16[96,768]{1,0:T(8,128)(2,1)S(1)}, u32[]{:S(2)}, u32[]{:S(2)}) collective-permute-start(bf16[96,768]{1,0:T(8,128)(2,1)S(1)} %convert_element_type.300), channel_id=1, source_target_pairs={{0,16},{1,17},{2,18},{3,19},{4,20},{5,21},{6,22},{7,23},{8,24},{9,... | collective-permute-start | bytes 442376 | tf_op jit(solution)/shard_map/ppermute | solution.py:36
  8.2 20.2 %collective-permute-start = (bf16[104,768]{1,0:T(8,128)(2,1)S(1)}, bf16[104,768]{1,0:T(8,128)(2,1)S(1)}, u32[]{:S(2)}, u32[]{:S(2)}) collective-permute-start(bf16[104,768]{1,0:T(8,128)(2,1)S(1)} %fusion.71), channel_id=1, source_target_pairs={{0,16},{1,17},{2,18},{3,19},{4,20},{5,21},{6,22},{7,23},{8,24},{9,... | collective-permute-start | bytes 479240 | tf_op jit(solution)/shard_map/ppermute | solution.py:36
  9.3 16.7 %collective-permute-start.5 = (bf16[24,3072]{1,0:T(8,128)(2,1)S(1)}, bf16[24,3072]{1,0:T(8,128)(2,1)S(1)}, u32[]{:S(2)}, u32[]{:S(2)}) collective-permute-start(bf16[24,3072]{1,0:T(8,128)(2,1)S(1)} %convert_element_type.298), channel_id=1, source_target_pairs={{0,16},{1,17},{2,18},{3,19},{4,20},{5,21},{6,22},{7,23},{8,24},{9,... | collective-permute-start | bytes 442376 | tf_op jit(solution)/shard_map/ppermute | solution.py:36
  26.1 10.0 %collective-permute-start.11 = (bf16[2,96,768]{2,1,0:T(8,128)(2,1)S(1)}, bf16[2,96,768]{2,1,0:T(8,128)(2,1)S(1)}, u32[]{:S(2)}, u32[]{:S(2)}) collective-permute-start(bf16[2,96,768]{2,1,0:T(8,128)(2,1)S(1)} %maximum_select_fusion.14), channel_id=1, source_target_pairs={{0,8},{1,9},{2,10},{3,11},{4,12},{5,13},{6,14},{7,15},{8,0},{9,1},... | collective-permute-start | bytes 884744 | tf_op jit(solution)/shard_map/ppermute | solution.py:36
  26.9 15.5 %collective-permute-start.6 = (bf16[2,24,3072]{2,1,0:T(8,128)(2,1)S(1)}, bf16[2,24,3072]{2,1,0:T(8,128)(2,1)S(1)}, u32[]{:S(2)}, u32[]{:S(2)}) collective-permute-start(bf16[2,24,3072]{2,1,0:T(8,128)(2,1)S(1)} %maximum_select_fusion.12), channel_id=1, source_target_pairs={{0,8},{1,9},{2,10},{3,11},{4,12},{5,13},{6,14},{7,15},{8,0},{9,1},... | collective-permute-start | bytes 884744 | tf_op jit(solution)/shard_map/ppermute | solution.py:36
  28.4 19.1 %collective-permute-start.1 = (bf16[2,104,768]{2,1,0:T(8,128)(2,1)S(1)}, bf16[2,104,768]{2,1,0:T(8,128)(2,1)S(1)}, u32[]{:S(2)}, u32[]{:S(2)}) collective-permute-start(bf16[2,104,768]{2,1,0:T(8,128)(2,1)S(1)} %maximum_select_fusion.10), channel_id=1, source_target_pairs={{0,8},{1,9},{2,10},{3,11},{4,12},{5,13},{6,14},{7,15},{8,0},{9,1},... | collective-permute-start | bytes 958472 | tf_op jit(solution)/shard_map/ppermute | solution.py:36
  36.2 13.0 %collective-permute-start.12 = (bf16[2,2,96,768]{3,2,1,0:T(8,128)(2,1)S(1)}, bf16[2,2,96,768]{3,2,1,0:T(8,128)(2,1)S(1)}, u32[]{:S(2)}, u32[]{:S(2)}) collective-permute-start(bf16[2,2,96,768]{3,2,1,0:T(8,128)(2,1)S(1)} %maximum_select_fusion.8), channel_id=1, source_target_pairs={{0,4},{1,3},{2,6},{3,1},{4,0},{5,7},{6,2},{7,5},{8,12},{9,11},{10,... | collective-permute-start | bytes 1769480 | tf_op jit(solution)/shard_map/ppermute | solution.py:36
  42.5 12.3 %collective-permute-start.7 = (bf16[2,2,24,3072]{3,2,1,0:T(8,128)(2,1)S(1)}, bf16[2,2,24,3072]{3,2,1,0:T(8,128)(2,1)S(1)}, u32[]{:S(2)}, u32[]{:S(2)}) collective-permute-start(bf16[2,2,24,3072]{3,2,1,0:T(8,128)(2,1)S(1)} %maximum_select_fusion.7), channel_id=1, source_target_pairs={{0,4},{1,3},{2,6},{3,1},{4,0},{5,7},{6,2},{7,5},{8,12},{9,11},{10,... | collective-permute-start | bytes 1769480 | tf_op jit(solution)/shard_map/ppermute | solution.py:36
  47.6 26.3 %collective-permute-start.2 = (bf16[2,2,104,768]{3,2,1,0:T(8,128)(2,1)S(1)}, bf16[2,2,104,768]{3,2,1,0:T(8,128)(2,1)S(1)}, u32[]{:S(2)}, u32[]{:S(2)}) collective-permute-start(bf16[2,2,104,768]{3,2,1,0:T(8,128)(2,1)S(1)} %maximum_select_fusion.6), channel_id=1, source_target_pairs={{0,4},{1,3},{2,6},{3,1},{4,0},{5,7},{6,2},{7,5},{8,12},{9,11},{10,... | collective-permute-start | bytes 1916936 | tf_op jit(solution)/shard_map/ppermute | solution.py:36
  49.1 24.8 %copy-start.22 = (bf16[1,2,2,104,768]{4,3,0,2,1:T(8,128)(2,1)}, bf16[1,2,2,104,768]{4,3,0,2,1:T(8,128)(2,1)S(1)}, u32[]{:S(2)}) copy-start(bf16[1,2,2,104,768]{4,3,0,2,1:T(8,128)(2,1)S(1)} %copy_select_fusion.3) | copy-start | bytes 1916932
  49.3 18.8 %collective-permute-start.13 = (bf16[2,2,2,96,768]{4,3,0,2,1:T(8,128)(2,1)S(1)}, bf16[2,2,2,96,768]{4,3,0,2,1:T(8,128)(2,1)S(1)}, u32[]{:S(2)}, u32[]{:S(2)}) collective-permute-start(bf16[2,2,2,96,768]{4,3,0,2,1:T(8,128)(2,1)S(1)} %maximum_select_fusion.5), channel_id=1, source_target_pairs={{0,2},{1,5},{2,0},{3,7},{4,6},{5,1},{6,4},{7,3},{8,10},{9,13},{10,... | collective-permute-start | bytes 3538952 | tf_op jit(solution)/shard_map/ppermute | solution.py:36
  54.9 25.8 %collective-permute-start.8 = (bf16[2,2,2,24,3072]{4,3,0,2,1:T(8,128)(2,1)S(1)}, bf16[2,2,2,24,3072]{4,3,0,2,1:T(8,128)(2,1)S(1)}, u32[]{:S(2)}, u32[]{:S(2)}) collective-permute-start(bf16[2,2,2,24,3072]{4,3,0,2,1:T(8,128)(2,1)S(1)} %maximum_select_fusion.4), channel_id=1, source_target_pairs={{0,2},{1,5},{2,0},{3,7},{4,6},{5,1},{6,4},{7,3},{8,10},{9,13},{10,... | collective-permute-start | bytes 3538952 | tf_op jit(solution)/shard_map/ppermute | solution.py:36
  69.8 30.8 %collective-permute-start.14 = (bf16[2,2,2,2,96,768]{5,4,1,0,3,2:T(8,128)(2,1)}, bf16[2,2,2,2,96,768]{5,4,1,0,3,2:T(8,128)(2,1)}, u32[]{:S(2)}, u32[]{:S(2)}) collective-permute-start(bf16[2,2,2,2,96,768]{5,4,1,0,3,2:T(8,128)(2,1)} %maximum_select_fusion.2), channel_id=1, source_target_pairs={{0,1},{1,0},{2,3},{3,2},{4,5},{5,4},{6,7},{7,6},{8,9},{9,8},{10,11... | collective-permute-start | bytes 7077896 | tf_op jit(solution)/shard_map/ppermute | solution.py:36
  75.1 19.4 %collective-permute-start.3 = (bf16[2,2,2,104,768]{4,3,0,2,1:T(8,128)(2,1)}, bf16[2,2,2,104,768]{4,3,0,2,1:T(8,128)(2,1)}, u32[]{:S(2)}, u32[]{:S(2)}) collective-permute-start(bf16[2,2,2,104,768]{4,3,0,2,1:T(8,128)(2,1)} %maximum_select_fusion.3), channel_id=1, source_target_pairs={{0,2},{1,5},{2,0},{3,7},{4,6},{5,1},{6,4},{7,3},{8,10},{9,13},{10,... | collective-permute-start | bytes 3833864 | tf_op jit(solution)/shard_map/ppermute | solution.py:36
  83.5 21.6 %collective-permute-start.9 = (bf16[2,2,2,2,24,3072]{5,4,1,0,3,2:T(8,128)(2,1)}, bf16[2,2,2,2,24,3072]{5,4,1,0,3,2:T(8,128)(2,1)}, u32[]{:S(2)}, u32[]{:S(2)}) collective-permute-start(bf16[2,2,2,2,24,3072]{5,4,1,0,3,2:T(8,128)(2,1)} %maximum_select_fusion.1), channel_id=1, source_target_pairs={{0,1},{1,0},{2,3},{3,2},{4,5},{5,4},{6,7},{7,6},{8,9},{9,8},{10,11... | collective-permute-start | bytes 7077896 | tf_op jit(solution)/shard_map/ppermute | solution.py:36
  88.8 57.6 %copy-start.18 = (pred[2,512,256]{1,2,0:T(8,128)(4,1)}, pred[2,512,256]{1,2,0:T(8,128)(4,1)S(1)}, u32[]{:S(2)}) copy-start(pred[2,512,256]{1,2,0:T(8,128)(4,1)S(1)} %broadcast_compare_fusion) | copy-start | bytes 786436
  96.9 12.7 %collective-permute-start.4 = (bf16[2,2,2,2,104,768]{5,4,1,0,3,2:T(8,128)(2,1)S(1)}, bf16[2,2,2,2,104,768]{5,4,1,0,3,2:T(8,128)(2,1)S(1)}, u32[]{:S(2)}, u32[]{:S(2)}) collective-permute-start(bf16[2,2,2,2,104,768]{5,4,1,0,3,2:T(8,128)(2,1)S(1)} %maximum_select_fusion), channel_id=1, source_target_pairs={{0,1},{1,0},{2,3},{3,2},{4,5},{5,4},{6,7},{7,6},{8,9},{9,8},{10,11... | collective-permute-start | bytes 7667720 | tf_op jit(solution)/shard_map/ppermute | solution.py:36
  155.7 38.2 %copy-start.6 = (f32[1024,768]{1,0:T(8,128)}, f32[1024,768]{1,0:T(8,128)S(1)}, u32[]{:S(2)}) copy-start(f32[1024,768]{1,0:T(8,128)S(1)} %get-tuple-element.109) | copy-start | bytes 9437188
  300.7 32.1 %collective-permute-start.25 = (bf16[2,2,2,2,96,768]{5,4,0,1,3,2:T(8,128)(2,1)}, bf16[2,2,2,2,96,768]{5,4,0,1,3,2:T(8,128)(2,1)}, u32[]{:S(2)}, u32[]{:S(2)}) collective-permute-start(bf16[2,2,2,2,96,768]{5,4,0,1,3,2:T(8,128)(2,1)} %bitcast.353), channel_id=1, source_target_pairs={{0,1},{1,0},{2,3},{3,2},{4,5},{5,4},{6,7},{7,6},{8,9},{9,8},{10,11... | collective-permute-start | bytes 7077896 | tf_op jit(solution)/shard_map/ppermute | solution.py:36
  315.5 23.7 %collective-permute-start.20 = (bf16[2,2,2,2,24,3072]{5,4,0,1,3,2:T(8,128)(2,1)}, bf16[2,2,2,2,24,3072]{5,4,0,1,3,2:T(8,128)(2,1)}, u32[]{:S(2)}, u32[]{:S(2)}) collective-permute-start(bf16[2,2,2,2,24,3072]{5,4,0,1,3,2:T(8,128)(2,1)} %bitcast.354), channel_id=1, source_target_pairs={{0,1},{1,0},{2,3},{3,2},{4,5},{5,4},{6,7},{7,6},{8,9},{9,8},{10,11... | collective-permute-start | bytes 7077896 | tf_op jit(solution)/shard_map/ppermute | solution.py:36
  332.6 17.2 %collective-permute-start.15 = (bf16[2,2,2,2,104,768]{5,4,3,2,1,0:T(8,128)(2,1)S(1)}, bf16[2,2,2,2,104,768]{5,4,3,2,1,0:T(8,128)(2,1)S(1)}, u32[]{:S(2)}, u32[]{:S(2)}) collective-permute-start(bf16[2,2,2,2,104,768]{5,4,3,2,1,0:T(8,128)(2,1)S(1)} %dynamic-slice_bitcast_fusion), channel_id=1, source_target_pairs={{0,1},{1,0},{2,3},{3,2},{4,5},{5,4},{6,7},{7,6},{8,9},{9,8},{10,11... | collective-permute-start | bytes 7667720 | tf_op jit(solution)/shard_map/ppermute | solution.py:36
  337.6 16.4 %collective-permute-start.26 = (bf16[2,2,2,96,768]{4,3,1,2,0:T(8,128)(2,1)}, bf16[2,2,2,96,768]{4,3,1,2,0:T(8,128)(2,1)S(1)}, u32[]{:S(2)}, u32[]{:S(2)}) collective-permute-start(bf16[2,2,2,96,768]{4,3,1,2,0:T(8,128)(2,1)} %fusion.45), channel_id=1, source_target_pairs={{0,2},{1,5},{2,0},{3,7},{4,6},{5,1},{6,4},{7,3},{8,10},{9,13},{10,... | collective-permute-start | bytes 3538952 | tf_op jit(solution)/shard_map/ppermute | solution.py:36
  343.1 30.0 %collective-permute-start.21 = (bf16[2,2,2,24,3072]{4,3,1,2,0:T(8,128)(2,1)}, bf16[2,2,2,24,3072]{4,3,1,2,0:T(8,128)(2,1)}, u32[]{:S(2)}, u32[]{:S(2)}) collective-permute-start(bf16[2,2,2,24,3072]{4,3,1,2,0:T(8,128)(2,1)} %fusion.46), channel_id=1, source_target_pairs={{0,2},{1,5},{2,0},{3,7},{4,6},{5,1},{6,4},{7,3},{8,10},{9,13},{10,... | collective-permute-start | bytes 3538952 | tf_op jit(solution)/shard_map/ppermute | solution.py:36
  350.7 42.4 %collective-permute-start.16 = (bf16[2,2,2,104,768]{4,3,0,2,1:T(8,128)(2,1)S(1)}, bf16[2,2,2,104,768]{4,3,0,2,1:T(8,128)(2,1)S(1)}, u32[]{:S(2)}, u32[]{:S(2)}) collective-permute-start(bf16[2,2,2,104,768]{4,3,0,2,1:T(8,128)(2,1)S(1)} %fusion.41), channel_id=1, source_target_pairs={{0,2},{1,5},{2,0},{3,7},{4,6},{5,1},{6,4},{7,3},{8,10},{9,13},{10,... | collective-permute-start | bytes 3833864 | tf_op jit(solution)/shard_map/ppermute | solution.py:36
  354.5 40.6 %collective-permute-start.27 = (bf16[2,2,96,768]{3,2,0,1:T(8,128)(2,1)S(1)}, bf16[2,2,96,768]{3,2,0,1:T(8,128)(2,1)S(1)}, u32[]{:S(2)}, u32[]{:S(2)}) collective-permute-start(bf16[2,2,96,768]{3,2,0,1:T(8,128)(2,1)S(1)} %fusion.53), channel_id=1, source_target_pairs={{0,4},{1,3},{2,6},{3,1},{4,0},{5,7},{6,2},{7,5},{8,12},{9,11},{10,... | collective-permute-start | bytes 1769480 | tf_op jit(solution)/shard_map/ppermute | solution.py:36
  375.0 21.0 %collective-permute-start.22 = (bf16[2,2,24,3072]{3,2,0,1:T(8,128)(2,1)S(1)}, bf16[2,2,24,3072]{3,2,0,1:T(8,128)(2,1)S(1)}, u32[]{:S(2)}, u32[]{:S(2)}) collective-permute-start(bf16[2,2,24,3072]{3,2,0,1:T(8,128)(2,1)S(1)} %fusion.52), channel_id=1, source_target_pairs={{0,4},{1,3},{2,6},{3,1},{4,0},{5,7},{6,2},{7,5},{8,12},{9,11},{10,... | collective-permute-start | bytes 1769480 | tf_op jit(solution)/shard_map/ppermute | solution.py:36
  393.5 17.8 %collective-permute-start.17 = (bf16[2,2,104,768]{3,2,1,0:T(8,128)(2,1)S(1)}, bf16[2,2,104,768]{3,2,1,0:T(8,128)(2,1)S(1)}, u32[]{:S(2)}, u32[]{:S(2)}) collective-permute-start(bf16[2,2,104,768]{3,2,1,0:T(8,128)(2,1)S(1)} %fusion.51), channel_id=1, source_target_pairs={{0,4},{1,3},{2,6},{3,1},{4,0},{5,7},{6,2},{7,5},{8,12},{9,11},{10,... | collective-permute-start | bytes 1916936 | tf_op jit(solution)/shard_map/ppermute | solution.py:36
  395.4 11.6 %collective-permute-start.28 = (bf16[2,96,768]{2,1,0:T(8,128)(2,1)S(1)}, bf16[2,96,768]{2,1,0:T(8,128)(2,1)S(1)}, u32[]{:S(2)}, u32[]{:S(2)}) collective-permute-start(bf16[2,96,768]{2,1,0:T(8,128)(2,1)S(1)} %fusion.65), channel_id=1, source_target_pairs={{0,8},{1,9},{2,10},{3,11},{4,12},{5,13},{6,14},{7,15},{8,0},{9,1},... | collective-permute-start | bytes 884744 | tf_op jit(solution)/shard_map/ppermute | solution.py:36
  396.2 15.0 %collective-permute-start.23 = (bf16[2,24,3072]{2,1,0:T(8,128)(2,1)S(1)}, bf16[2,24,3072]{2,1,0:T(8,128)(2,1)S(1)}, u32[]{:S(2)}, u32[]{:S(2)}) collective-permute-start(bf16[2,24,3072]{2,1,0:T(8,128)(2,1)S(1)} %fusion.64), channel_id=1, source_target_pairs={{0,8},{1,9},{2,10},{3,11},{4,12},{5,13},{6,14},{7,15},{8,0},{9,1},... | collective-permute-start | bytes 884744 | tf_op jit(solution)/shard_map/ppermute | solution.py:36
  407.1 8.9 %collective-permute-start.29 = (bf16[96,768]{1,0:T(8,128)(2,1)S(1)}, bf16[96,768]{1,0:T(8,128)(2,1)S(1)}, u32[]{:S(2)}, u32[]{:S(2)}) collective-permute-start(bf16[96,768]{1,0:T(8,128)(2,1)S(1)} %fusion.74), channel_id=1, source_target_pairs={{0,16},{1,17},{2,18},{3,19},{4,20},{5,21},{6,22},{7,23},{8,24},{9,... | collective-permute-start | bytes 442376 | tf_op jit(solution)/shard_map/ppermute | solution.py:36
  411.5 12.0 %collective-permute-start.18 = (bf16[2,104,768]{2,1,0:T(8,128)(2,1)S(1)}, bf16[2,104,768]{2,1,0:T(8,128)(2,1)S(1)}, u32[]{:S(2)}, u32[]{:S(2)}) collective-permute-start(bf16[2,104,768]{2,1,0:T(8,128)(2,1)S(1)} %fusion.57), channel_id=1, source_target_pairs={{0,8},{1,9},{2,10},{3,11},{4,12},{5,13},{6,14},{7,15},{8,0},{9,1},... | collective-permute-start | bytes 958472 | tf_op jit(solution)/shard_map/ppermute | solution.py:36
  412.2 20.8 %copy-start.59 = (f32[8,512]{1,0:T(8,128)S(1)}, f32[8,512]{1,0:T(8,128)}, u32[]{:S(2)}) copy-start(f32[8,512]{1,0:T(8,128)} %param.34) | copy-start | bytes 49156
  412.2 20.8 %copy-start.67 = (f32[8,512]{1,0:T(8,128)S(1)}, f32[8,512]{1,0:T(8,128)}, u32[]{:S(2)}) copy-start(f32[8,512]{1,0:T(8,128)} %param.35) | copy-start | bytes 49156
  412.2 20.8 %copy-start.68 = (f32[8,512]{1,0:T(8,128)S(1)}, f32[8,512]{1,0:T(8,128)}, u32[]{:S(2)}) copy-start(f32[8,512]{1,0:T(8,128)} %param.36) | copy-start | bytes 49156
  412.2 21.4 %copy-start.35 = (f32[4,24,768]{2,1,0:T(8,128)S(1)}, f32[4,24,768]{2,1,0:T(8,128)}, u32[]{:S(2)}) copy-start(f32[4,24,768]{2,1,0:T(8,128)} %param.25) | copy-start | bytes 884740
  412.2 21.4 %copy-start.55 = (f32[4,24,768]{2,1,0:T(8,128)S(1)}, f32[4,24,768]{2,1,0:T(8,128)}, u32[]{:S(2)}) copy-start(f32[4,24,768]{2,1,0:T(8,128)} %param.27) | copy-start | bytes 884740
  412.3 21.4 %copy-start.56 = (f32[4,24,768]{2,1,0:T(8,128)S(1)}, f32[4,24,768]{2,1,0:T(8,128)}, u32[]{:S(2)}) copy-start(f32[4,24,768]{2,1,0:T(8,128)} %param.26) | copy-start | bytes 884740
  412.3 12.9 %collective-permute-start.24 = (bf16[24,3072]{1,0:T(8,128)(2,1)S(1)}, bf16[24,3072]{1,0:T(8,128)(2,1)S(1)}, u32[]{:S(2)}, u32[]{:S(2)}) collective-permute-start(bf16[24,3072]{1,0:T(8,128)(2,1)S(1)} %fusion.73), channel_id=1, source_target_pairs={{0,16},{1,17},{2,18},{3,19},{4,20},{5,21},{6,22},{7,23},{8,24},{9,... | collective-permute-start | bytes 442376 | tf_op jit(solution)/shard_map/ppermute | solution.py:36
  417.0 39.4 %copy-start.42 = (f32[96,768]{1,0:T(8,128)}, f32[96,768]{1,0:T(8,128)S(1)}, u32[]{:S(2)}) copy-start(f32[96,768]{1,0:T(8,128)S(1)} %get-tuple-element.66) | copy-start | bytes 884740
  417.0 39.4 %copy-start.43 = (f32[96,768]{1,0:T(8,128)}, f32[96,768]{1,0:T(8,128)S(1)}, u32[]{:S(2)}) copy-start(f32[96,768]{1,0:T(8,128)S(1)} %get-tuple-element.67) | copy-start | bytes 884740
  423.6 19.7 %copy-start.69 = (f32[4,24]{1,0:T(4,128)S(1)}, f32[4,24]{1,0:T(4,128)}, u32[]{:S(2)}) copy-start(f32[4,24]{1,0:T(4,128)} %param.37) | copy-start | bytes 1156
  423.6 9.3 %collective-permute-start.19 = (bf16[104,768]{1,0:T(8,128)(2,1)S(1)}, bf16[104,768]{1,0:T(8,128)(2,1)S(1)}, u32[]{:S(2)}, u32[]{:S(2)}) collective-permute-start(bf16[104,768]{1,0:T(8,128)(2,1)S(1)} %fusion.72), channel_id=1, source_target_pairs={{0,16},{1,17},{2,18},{3,19},{4,20},{5,21},{6,22},{7,23},{8,24},{9,... | collective-permute-start | bytes 479240 | tf_op jit(solution)/shard_map/ppermute | solution.py:36
  426.2 31.1 %copy-start.44 = (f32[24,3072]{1,0:T(8,128)}, f32[24,3072]{1,0:T(8,128)S(1)}, u32[]{:S(2)}) copy-start(f32[24,3072]{1,0:T(8,128)S(1)} %get-tuple-element.68) | copy-start | bytes 884740
  426.2 31.1 %copy-start.45 = (f32[24,3072]{1,0:T(8,128)}, f32[24,3072]{1,0:T(8,128)S(1)}, u32[]{:S(2)}) copy-start(f32[24,3072]{1,0:T(8,128)S(1)} %get-tuple-element.69) | copy-start | bytes 884740
  433.7 24.6 %copy-start.60 = (f32[8,512]{1,0:T(8,128)}, f32[8,512]{1,0:T(8,128)S(1)}, u32[]{:S(2)}) copy-start(f32[8,512]{1,0:T(8,128)S(1)} %get-tuple-element.64) | copy-start | bytes 49156
  433.7 24.6 %copy-start.61 = (f32[8,512]{1,0:T(8,128)}, f32[8,512]{1,0:T(8,128)S(1)}, u32[]{:S(2)}) copy-start(f32[8,512]{1,0:T(8,128)S(1)} %get-tuple-element.65) | copy-start | bytes 49156
  434.1 24.2 %copy-start.46 = (f32[4,24,768]{2,1,0:T(8,128)}, f32[4,24,768]{2,1,0:T(8,128)S(1)}, u32[]{:S(2)}) copy-start(f32[4,24,768]{2,1,0:T(8,128)S(1)} %get-tuple-element.71) | copy-start | bytes 884740
  438.7 12.8 %all-to-all-start = ((f32[32,8,128]{2,1,0:T(8,128)}), f32[32,8,128]{2,1,0:T(8,128)S(1)}, u32[]{:S(2)}, u32[]{:S(2)}) async-start(f32[32,8,128]{2,1,0:T(8,128)} %broadcast_in_dim.66), calls=%async_computation | async-start | bytes 262144 | tf_op jit(solution)/shard_map/all_to_all | solution.py:99
  (67 other events, 453.8 us)
